TPU v7x, 512 devices: a whole 4x4x16 slice. The times are simulated.
512 devices in a mesh: wide: 32 (over z, core), narrow: 16 (over x, y).
Axes of the slice: x: 4, y: 4, z: 16, core: 2. Of those that a mesh axis runs over, the one named last changes fastest.
Arguments:
- activations: bfloat16 [512, 16384], P(None, 'wide'), may hold values from -6 to 6
- enc_weight: bfloat16 [16384, 16384], P('wide', 'narrow'), may hold values from -0.046875 to 0.046875
- enc_bias: float32 [16384], P('narrow'), may hold values from -4 to 4
- dec_weight: bfloat16 [16384, 16384], P('narrow', 'wide'), may hold values from -0.375 to 0.375
- dec_bias: float32 [16384], P('wide'), may hold values from -4 to 4
- active_ids: int32 [512, 64], replicated, may hold values from 0 to 16383, all different within a row
Outputs:
- dec_grad: bfloat16 [16384, 16384], P('narrow', 'wide')
- latent_grad: float32 [512, 16384], P('wide', 'narrow')
Inputs may be any that keep to these rules, and one draw needn't show every extreme that they name: `active_ids`: each row names 64 different latents; every latent is named by some row.
All inputs are finite; a program needn't handle non-finite values.
Results may differ from a plain program's by a relative error of at most 0.0058.
Values may be sent and summed in bfloat16 or wider, within the bound.
No kernel may reach another device: no remote copies, remote signals or barrier semaphores. Data moves between devices by JAX's collectives and lax.ppermute only.
A program may use at most 128 MiB of HBM per device.

v0:
```python
import jax
import jax.numpy as jnp
from jax import lax
from jax.sharding import Mesh
from jax.sharding import PartitionSpec as P

NARROW = ("narrow_0", "narrow_1")
WIDE = ("wide_0", "wide_1")


def filled_with(value, identity):
    return jnp.broadcast_to(jnp.asarray(identity, value.dtype), value.shape)


def carried_in(value, axes, combine, identity, reverse):
    before = start = filled_with(value, identity)
    total = value
    for axis in reversed(axes):
        length, position = (lax.axis_size(axis), lax.axis_index(axis))
        pieces = lax.all_gather(total, axis)
        inside, total = (start, start)
        for k in reversed(range(length)) if reverse else range(length):
            passed = k > position if reverse else k < position
            total = combine(total, pieces[k])
            inside = jnp.where(passed, total, inside)
        before = combine(inside, before)
    return before


def reduced_to_own(pieces, axes, turns):
    inside = pieces.shape[1:]
    pieces = pieces.reshape(*(lax.axis_size(a) for a in axes), *inside)
    pieces = jnp.moveaxis(pieces, turns, range(len(axes))).reshape(-1, *inside)
    for k in turns:
        pieces = lax.psum_scatter(pieces, axes[k], scatter_dimension=0, tiled=True)
    return pieces[0]


def in_blocks(value, dim, length):
    dims = value.shape
    pieces = value.reshape(*dims[:dim], length, dims[dim] // length, *dims[dim + 1 :])
    return jnp.moveaxis(pieces, dim, 0)


def summed_rows(value, axes, turns, dim):
    length = lax.axis_size(axes)
    return reduced_to_own(in_blocks(value, dim, length), axes, turns)


def add_fields(earlier, later):
    return jax.tree.map(jnp.add, earlier, later)


def local(activations, enc_weight, enc_bias, dec_weight, dec_bias, active_ids):
    token_count = activations.shape[0]
    latent_width = enc_weight.shape[1]
    groups = lax.axis_size(NARROW)
    group_index = lax.axis_index(NARROW)
    first_latent = group_index * latent_width
    inside = (active_ids >= first_latent) & (active_ids < first_latent + latent_width)
    local_ids = jnp.where(inside, active_ids - first_latent, latent_width)
    row_index = jnp.arange(token_count, dtype=jnp.int32)[:, None]
    active_mask = (
        jnp.zeros((token_count, latent_width), jnp.float32)
        .at[row_index, local_ids]
        .set(1.0, mode="drop")
    )
    share_rows = token_count // lax.axis_size(WIDE)
    offset = lax.axis_index(WIDE) * share_rows
    own_mask = lax.dynamic_slice_in_dim(active_mask, offset, share_rows, 0)
    partial_pre = jnp.dot(activations, enc_weight, preferred_element_type=jnp.float32)
    preact = lax.psum(partial_pre, WIDE) + enc_bias
    latents = (active_mask * preact).astype(jnp.bfloat16)
    recon_part = jnp.dot(latents, dec_weight, preferred_element_type=jnp.float32)
    target = activations.astype(jnp.float32)
    nothing = jnp.zeros_like(recon_part)
    before = carried_in(recon_part, NARROW, add_fields, nothing, False)
    errors_here = dec_bias + before + recon_part - target
    later_sum = carried_in(errors_here, NARROW, add_fields, nothing, True)
    suffix = later_sum + errors_here
    errors = (suffix / groups).astype(jnp.bfloat16)
    dec_grad = lax.dot_general(
        latents, errors, (((0,), (0,)), ((), ())), preferred_element_type=jnp.float32
    ).astype(jnp.bfloat16)
    latent_rows = summed_rows(
        lax.dot_general(
            errors, dec_weight, (((1,), (1,)), ((), ())), preferred_element_type=jnp.float32
        ),
        WIDE,
        (1, 0),
        0,
    )
    latent_out = own_mask * latent_rows
    return (dec_grad, latent_out)


def solution(mesh):
    split = Mesh(mesh.devices.reshape(16, 2, 4, 4), ("wide_0", "wide_1", "narrow_0", "narrow_1"))
    return jax.shard_map(
        local,
        mesh=split,
        in_specs=(P(None, WIDE), P(WIDE, NARROW), P(NARROW), P(NARROW, WIDE), P(WIDE), P()),
        out_specs=(P(NARROW, WIDE), P(WIDE, NARROW)),
        check_vma=False,
    )
```

profile of v0, /device:TPU:2, one launch (start us, length us, event | category | flops | bytes accessed | tf_op | source)
XLA Modules:
  0.0 583.1 jit_solution(8263159260602203690)
XLA Ops:
  7.2 3.5 fusion.17
  10.9 0.5 copy-done.11
  11.5 0.1 and_reduce_fusion
  11.7 0.1 copy.10
  11.9 121.5 %scatter_custom_fusion = f32[524288]{0:T(1024)} fusion(s32[32768]{0:T(1024)S(1)} %reshape.66, f32[32768]{0:T(1024)S(1)} %broadcast.52, f32[]{:T(128)} %constant.17.clone.1), kind=kCustom, calls=%fused_computation.31 | custom fusion | bytes 2097156
  133.4 1.7 reshape.63
  135.1 94.1 %all-reduce.2.cloned.1.call-done = f32[512,1024]{1,0:T(8,128)} async-done(((f32[512,1024]{1,0:T(8,128)}), f32[512,1024]{1,0:T(8,128)}) %all-reduce.2.cloned.1.call-update) | async-done | bytes 2097168 | tf_op jit(solution)/shard_map/psum | solution.py:72
  229.2 2.1 multiply_convert_fusion
  231.3 1.0 copy-done.5
  232.3 1.7 fusion.18
  234.1 56.1 %all-gather.11.cloned.1.call-done = f32[2048,512]{1,0:T(8,128)} async-done(((f32[512,512]{1,0:T(8,128)}), f32[2048,512]{1,0:T(8,128)}) %all-gather.11.cloned.1.call-update) | async-done | bytes 4194320 | tf_op jit(solution)/shard_map/all_gather | solution.py:20
  290.1 3.7 fusion.13
  293.9 55.8 %all-gather.7.cloned.1.call-done = f32[4,512,512]{2,1,0:T(8,128)} async-done(((f32[1,512,512]{2,1,0:T(8,128)}), f32[4,512,512]{2,1,0:T(8,128)}) %all-gather.7.cloned.1.call-update) | async-done | bytes 4194320 | tf_op jit(solution)/shard_map/all_gather | solution.py:20
  349.7 5.6 fusion.12
  355.4 57.1 %all-gather.13.cloned.1.call-done = f32[2048,512]{1,0:T(8,128)} async-done(((f32[512,512]{1,0:T(8,128)}), f32[2048,512]{1,0:T(8,128)}) %all-gather.13.cloned.1.call-update) | async-done | bytes 4194320 | tf_op jit(solution)/shard_map/all_gather | solution.py:20
  412.5 3.7 fusion.6
  416.2 55.8 %all-gather.9.cloned.1.call-done = f32[4,512,512]{2,1,0:T(8,128)} async-done(((f32[1,512,512]{2,1,0:T(8,128)}), f32[4,512,512]{2,1,0:T(8,128)}) %all-gather.9.cloned.1.call-update) | async-done | bytes 4194320 | tf_op jit(solution)/shard_map/all_gather | solution.py:20
  472.0 4.6 fusion.5
  476.6 0.7 fusion.19
  477.4 1.5 copy.11
  478.9 21.2 %reduce-scatter.3.cloned.1.call-done = f32[16,16,1024]{2,1,0:T(8,128)} async-done(((f32[32,16,1024]{2,1,0:T(8,128)}), f32[16,16,1024]{2,1,0:T(8,128)}) %reduce-scatter.3.cloned.1.call-update) | async-done | bytes 1048592 | tf_op jit(solution)/shard_map/reduce_scatter | solution.py:35
  500.2 1.7 convolution_convert_fusion
  501.9 72.8 %reduce-scatter.5.cloned.1.call-done = f32[1,16,1024]{2,1,0:T(8,128)} async-done(((f32[16,16,1024]{2,1,0:T(8,128)}), f32[1,16,1024]{2,1,0:T(8,128)}) %reduce-scatter.5.cloned.1.call-update) | async-done | bytes 65552 | tf_op jit(solution)/shard_map/reduce_scatter | solution.py:35
  574.7 1.5 bitcast_multiply_fusion
  (42 shorter events, 0.7 us)
Async XLA Ops:
  7.2 225.1 %copy-start = (bf16[1024,512]{1,0:T(8,128)(2,1)S(1)}, bf16[1024,512]{1,0:T(8,128)(2,1)}, u32[]{:S(2)}) copy-start(bf16[1024,512]{1,0:T(8,128)(2,1)} %param.9) | copy-start | bytes 3145732
  7.2 3.7 copy-start.7
  7.2 222.0 %all-reduce.2.cloned.1.call-start = ((), (), s32[]{:S(2)}) async-start(), calls=%async_computation.2 | async-start | bytes 4194304 | tf_op jit(solution)/shard_map/psum | solution.py:72
  10.8 0.7 copy-start.11
  10.8 0.7 copy-start.10
  10.8 279.3 %all-gather.11.cloned.1.call-start = ((), (), s32[]{:S(2)}) async-start(), calls=%async_computation.7 | async-start | bytes 5242880 | tf_op jit(solution)/shard_map/all_gather | solution.py:20
  133.4 95.8 %copy-start.8 = (f32[1024]{0:T(1024)S(1)}, f32[1024]{0:T(1024)}, u32[]{:S(2)}) copy-start(f32[1024]{0:T(1024)} %param.8) | copy-start | bytes 12292
  135.1 96.2 %copy-start.2 = (f32[512,1024]{1,0:T(8,128)}, f32[512,1024]{1,0:T(8,128)S(1)}, u32[]{:S(2)}) copy-start(f32[512,1024]{1,0:T(8,128)S(1)} %reshape.63) | copy-start | bytes 6291460
  231.3 1.0 copy-start.5
  234.0 115.7 %copy-start.3 = (f32[512,512]{1,0:T(8,128)S(1)}, f32[512,512]{1,0:T(8,128)}, u32[]{:S(2)}) copy-start(f32[512,512]{1,0:T(8,128)} %fusion.18) | copy-start | bytes 3145732
  234.0 115.7 %copy-start.4 = (bf16[512,512]{1,0:T(8,128)(2,1)S(1)}, bf16[512,512]{1,0:T(8,128)(2,1)}, u32[]{:S(2)}) copy-start(bf16[512,512]{1,0:T(8,128)(2,1)} %param.6) | copy-start | bytes 1572868
  234.0 115.7 %copy-start.9 = (f32[512]{0:T(512)S(1)}, f32[512]{0:T(512)}, u32[]{:S(2)}) copy-start(f32[512]{0:T(512)} %param.10) | copy-start | bytes 6148
  234.0 115.6 %all-gather.7.cloned.1.call-start = ((), (), s32[]{:S(2)}) async-start(), calls=%async_computation.3 | async-start | bytes 5242880 | tf_op jit(solution)/shard_map/all_gather | solution.py:20
  293.8 118.7 %all-gather.13.cloned.1.call-start = ((), (), s32[]{:S(2)}) async-start(), calls=%async_computation.8 | async-start | bytes 5242880 | tf_op jit(solution)/shard_map/all_gather | solution.py:20
  355.3 116.7 %copy-start.1 = (f32[512,512]{1,0:T(8,128)S(1)}, f32[512,512]{1,0:T(8,128)}, u32[]{:S(2)}) copy-start(f32[512,512]{1,0:T(8,128)} %fusion.12) | copy-start | bytes 3145732
  355.3 116.7 %all-gather.9.cloned.1.call-start = ((), (), s32[]{:S(2)}) async-start(), calls=%async_computation.4 | async-start | bytes 5242880 | tf_op jit(solution)/shard_map/all_gather | solution.py:20
  416.2 84.0 %reduce-scatter.3.cloned.1.call-start = ((), (), s32[]{:S(2)}) async-start(), calls=%async_computation.5 | async-start | bytes 3145728 | tf_op jit(solution)/shard_map/reduce_scatter | solution.py:35
  478.8 21.3 %copy-start.6 = (bf16[512,1024]{1,0:T(8,128)(2,1)S(1)}, bf16[512,1024]{1,0:T(8,128)(2,1)}, u32[]{:S(2)}) copy-start(bf16[512,1024]{1,0:T(8,128)(2,1)} %copy-done.5) | copy-start | bytes 3145732
  478.9 95.9 %reduce-scatter.5.cloned.1.call-start = ((), (), s32[]{:S(2)}) async-start(), calls=%async_computation.6 | async-start | bytes 1114112 | tf_op jit(solution)/shard_map/reduce_scatter | solution.py:35
Sparse Core Ops, SparseCore 0:
  10.9 218.2 all-reduce.1
  234.1 55.9 all-gather.10
  293.9 55.6 all-gather.6
  355.4 57.0 all-gather.12
  416.3 55.6 all-gather.8
  479.0 21.1 reduce-scatter.2
  502.9 71.7 reduce-scatter.4
where the time goes:
time: 583 us
  waiting for transfers between devices  413 us (71%)
  local copies, waits for them, and re-layouts  126 us (22%)
  other arithmetic  21.4 us (4%)
  between operations  14.3 us (2%)
  matrix products  7.66 us (1%)
    all_gather x4, waiting for transfers between devices, carried_in(): pieces = lax.all_gather(total, axis)  225 us
    unnamed x28, local copies, waits for them, and re-layouts  123 us
    reduce_scatter x2, waiting for transfers between devices, reduced_to_own(): pieces = lax.psum_scatter(pieces, axes[k], scatter_dimension=0, tiled=True)  94.1 us
    psum x1, waiting for transfers between devices, local(): preact = lax.psum(partial_pre, WIDE) + enc_bias  94.1 us
  transfers between devices with their start and end apart: 7, of which 7 were waited for; matrix products, arithmetic and copies ran while one was open for 22% of the time, Pallas kernels for 0%

commit v1 on v0

--- a/solution.py
+++ b/solution.py
@@ -6,6 +6,7 @@
 
 NARROW = ("narrow_0", "narrow_1")
 WIDE = ("wide_0", "wide_1")
+apply_the_rails = lambda state, mesh_dim: jnp.sum(lax.all_gather(state, mesh_dim), axis=0)
 
 
 def filled_with(value, identity):
@@ -69,7 +70,7 @@
     offset = lax.axis_index(WIDE) * share_rows
     own_mask = lax.dynamic_slice_in_dim(active_mask, offset, share_rows, 0)
     partial_pre = jnp.dot(activations, enc_weight, preferred_element_type=jnp.float32)
-    preact = lax.psum(partial_pre, WIDE) + enc_bias
+    preact = apply_the_rails(partial_pre, WIDE) + enc_bias
     latents = (active_mask * preact).astype(jnp.bfloat16)
     recon_part = jnp.dot(latents, dec_weight, preferred_element_type=jnp.float32)
     target = activations.astype(jnp.float32)

time: 583 us -> 750 us (1.29)
  the two profiles are of different devices: /device:TPU:2 before, /device:TPU:4 now
where the time goes in v1:
time: 750 us
  waiting for transfers between devices  557 us (74%)
  local copies, waits for them, and re-layouts  126 us (17%)
  other arithmetic  43.6 us (6%)
  between operations  14.3 us (2%)
  matrix products  7.78 us (1%)
    all_gather x1, waiting for transfers between devices, lax.all_gather(state, mesh_dim)  240 us
    all_gather x4, waiting for transfers between devices, carried_in(): pieces = lax.all_gather(total, axis)  222 us
    unnamed x28, local copies, waits for them, and re-layouts  123 us
    reduce_scatter x2, waiting for transfers between devices, reduced_to_own(): pieces = lax.psum_scatter(pieces, axes[k], scatter_dimension=0, tiled=True)  94.6 us
    reduce_sum x1, other arithmetic, jnp.sum(lax.all_gather(state, mesh_dim), axis=0)  22.2 us
  transfers between devices with their start and end apart: 7, of which 7 were waited for; matrix products, arithmetic and copies ran while one was open for 17% of the time, Pallas kernels for 0%

profile of v1, /device:TPU:4, one launch (start us, length us, event | category | flops | bytes accessed | tf_op | source)
XLA Modules:
  0.0 749.8 jit_solution(4290130528920797497)
XLA Ops:
  7.2 3.6 fusion.17
  11.0 0.5 copy-done.11
  11.7 0.1 copy.10
  11.9 121.5 %scatter_custom_fusion = f32[524288]{0:T(1024)} fusion(s32[32768]{0:T(1024)S(1)} %reshape.66, f32[32768]{0:T(1024)S(1)} %broadcast.52, f32[]{:T(128)} %constant.17.clone.1), kind=kCustom, calls=%fused_computation.31 | custom fusion | bytes 2097156
  133.4 1.8 reshape.63
  135.2 240.3 %all-gather.13.cloned.1.call-done = f32[16384,1024]{1,0:T(8,128)} async-done(((f32[512,1024]{1,0:T(8,128)}), f32[16384,1024]{1,0:T(8,128)}) %all-gather.13.cloned.1.call-update) | async-done | bytes 67108880 | tf_op jit(solution)/shard_map/all_gather | solution.py:9
  375.5 22.2 %reduce_sum.9 = f32[512,1024]{1,0:T(8,128)} reduce(f32[32,512,1024]{2,1,0:T(8,128)} %bitcast.1, f32[]{:T(128)} %constant.17.clone.1), dimensions={0}, to_apply=%region_1.2 | reduce | flops 16252928 | bytes 69206016 | tf_op jit(solution)/shard_map/reduce_sum | solution.py:9
  397.7 2.1 multiply_convert_fusion
  399.8 1.0 copy-done.5
  400.7 1.8 fusion.18
  402.6 53.9 %all-gather.15.cloned.1.call-done = f32[2048,512]{1,0:T(8,128)} async-done(((f32[512,512]{1,0:T(8,128)}), f32[2048,512]{1,0:T(8,128)}) %all-gather.15.cloned.1.call-update) | async-done | bytes 4194320 | tf_op jit(solution)/shard_map/all_gather | solution.py:21
  456.6 3.6 fusion.13
  460.3 55.5 %all-gather.9.cloned.1.call-done = f32[4,512,512]{2,1,0:T(8,128)} async-done(((f32[1,512,512]{2,1,0:T(8,128)}), f32[4,512,512]{2,1,0:T(8,128)}) %all-gather.9.cloned.1.call-update) | async-done | bytes 4194320 | tf_op jit(solution)/shard_map/all_gather | solution.py:21
  515.8 5.7 fusion.12
  521.6 57.4 %all-gather.17.cloned.1.call-done = f32[2048,512]{1,0:T(8,128)} async-done(((f32[512,512]{1,0:T(8,128)}), f32[2048,512]{1,0:T(8,128)}) %all-gather.17.cloned.1.call-update) | async-done | bytes 4194320 | tf_op jit(solution)/shard_map/all_gather | solution.py:21
  579.0 3.6 fusion.6
  582.7 55.5 %all-gather.11.cloned.1.call-done = f32[4,512,512]{2,1,0:T(8,128)} async-done(((f32[1,512,512]{2,1,0:T(8,128)}), f32[4,512,512]{2,1,0:T(8,128)}) %all-gather.11.cloned.1.call-update) | async-done | bytes 4194320 | tf_op jit(solution)/shard_map/all_gather | solution.py:21
  638.2 4.6 fusion.5
  642.8 0.7 fusion.19
  643.5 1.5 copy.11
  645.1 21.5 %reduce-scatter.3.cloned.1.call-done = f32[16,16,1024]{2,1,0:T(8,128)} async-done(((f32[32,16,1024]{2,1,0:T(8,128)}), f32[16,16,1024]{2,1,0:T(8,128)}) %reduce-scatter.3.cloned.1.call-update) | async-done | bytes 1048592 | tf_op jit(solution)/shard_map/reduce_scatter | solution.py:36
  666.6 1.7 convolution_convert_fusion
  668.3 73.1 %reduce-scatter.5.cloned.1.call-done = f32[1,16,1024]{2,1,0:T(8,128)} async-done(((f32[16,16,1024]{2,1,0:T(8,128)}), f32[1,16,1024]{2,1,0:T(8,128)}) %reduce-scatter.5.cloned.1.call-update) | async-done | bytes 65552 | tf_op jit(solution)/shard_map/reduce_scatter | solution.py:36
  741.5 1.5 bitcast_multiply_fusion
  (43 shorter events, 0.8 us)
Async XLA Ops:
  7.2 393.6 %copy-start = (bf16[1024,512]{1,0:T(8,128)(2,1)S(1)}, bf16[1024,512]{1,0:T(8,128)(2,1)}, u32[]{:S(2)}) copy-start(bf16[1024,512]{1,0:T(8,128)(2,1)} %param.9) | copy-start | bytes 3145732
  7.2 3.7 copy-start.7
  7.2 368.3 %all-gather.13.cloned.1.call-start = ((), (), s32[]{:S(2)}) async-start(), calls=%async_computation.6 | async-start | bytes 69206016 | tf_op jit(solution)/shard_map/all_gather | solution.py:9
  10.8 0.7 copy-start.11
  10.8 0.7 copy-start.10
  10.8 445.7 %all-gather.15.cloned.1.call-start = ((), (), s32[]{:S(2)}) async-start(), calls=%async_computation.7 | async-start | bytes 5242880 | tf_op jit(solution)/shard_map/all_gather | solution.py:21
  135.2 262.5 %copy-start.2 = (f32[512,1024]{1,0:T(8,128)}, f32[512,1024]{1,0:T(8,128)S(1)}, u32[]{:S(2)}) copy-start(f32[512,1024]{1,0:T(8,128)S(1)} %reshape.63) | copy-start | bytes 6291460
  375.5 22.2 %copy-start.8 = (f32[1024]{0:T(1024)S(1)}, f32[1024]{0:T(1024)}, u32[]{:S(2)}) copy-start(f32[1024]{0:T(1024)} %param.8) | copy-start | bytes 12292
  399.8 1.0 copy-start.5
  402.5 113.2 %copy-start.3 = (f32[512,512]{1,0:T(8,128)S(1)}, f32[512,512]{1,0:T(8,128)}, u32[]{:S(2)}) copy-start(f32[512,512]{1,0:T(8,128)} %fusion.18) | copy-start | bytes 3145732
  402.5 113.2 %copy-start.4 = (bf16[512,512]{1,0:T(8,128)(2,1)S(1)}, bf16[512,512]{1,0:T(8,128)(2,1)}, u32[]{:S(2)}) copy-start(bf16[512,512]{1,0:T(8,128)(2,1)} %param.6) | copy-start | bytes 1572868
  402.6 113.2 %copy-start.9 = (f32[512]{0:T(512)S(1)}, f32[512]{0:T(512)}, u32[]{:S(2)}) copy-start(f32[512]{0:T(512)} %param.10) | copy-start | bytes 6148
  402.6 113.2 %all-gather.9.cloned.1.call-start = ((), (), s32[]{:S(2)}) async-start(), calls=%async_computation.2 | async-start | bytes 5242880 | tf_op jit(solution)/shard_map/all_gather | solution.py:21
  460.2 118.7 %all-gather.17.cloned.1.call-start = ((), (), s32[]{:S(2)}) async-start(), calls=%async_computation.8 | async-start | bytes 5242880 | tf_op jit(solution)/shard_map/all_gather | solution.py:21
  521.5 116.7 %copy-start.1 = (f32[512,512]{1,0:T(8,128)S(1)}, f32[512,512]{1,0:T(8,128)}, u32[]{:S(2)}) copy-start(f32[512,512]{1,0:T(8,128)} %fusion.12) | copy-start | bytes 3145732
  521.5 116.7 %all-gather.11.cloned.1.call-start = ((), (), s32[]{:S(2)}) async-start(), calls=%async_computation.3 | async-start | bytes 5242880 | tf_op jit(solution)/shard_map/all_gather | solution.py:21
  582.6 84.0 %reduce-scatter.3.cloned.1.call-start = ((), (), s32[]{:S(2)}) async-start(), calls=%async_computation.4 | async-start | bytes 3145728 | tf_op jit(solution)/shard_map/reduce_scatter | solution.py:36
  645.0 21.6 %copy-start.6 = (bf16[512,1024]{1,0:T(8,128)(2,1)S(1)}, bf16[512,1024]{1,0:T(8,128)(2,1)}, u32[]{:S(2)}) copy-start(bf16[512,1024]{1,0:T(8,128)(2,1)} %copy-done.5) | copy-start | bytes 3145732
  645.0 96.4 %reduce-scatter.5.cloned.1.call-start = ((), (), s32[]{:S(2)}) async-start(), calls=%async_computation.5 | async-start | bytes 1114112 | tf_op jit(solution)/shard_map/reduce_scatter | solution.py:36
Sparse Core Ops, SparseCore 0:
  10.9 364.5 all-gather.12
  402.7 53.8 all-gather.14
  460.3 55.3 all-gather.8
  521.6 57.2 all-gather.16
  582.7 55.3 all-gather.10
  645.1 21.3 reduce-scatter.2
  669.6 71.7 reduce-scatter.4
